TPU v7x, 256 devices: a whole 4x4x8 slice. The times are simulated.
256 devices in a mesh: gx: 32 (over z, x), gy: 8 (over y, core).
Axes of the slice: x: 4, y: 4, z: 8, core: 2. Of those that a mesh axis runs over, the one named last changes fastest.
Arguments:
- velocity: float32 [3, 8, 1536, 8192], P(None, None, 'gy', 'gx'), may hold values from -6 to 6
- metric_x: float32 [8192], P('gx'), may hold values from 0.3 to 3
- metric_y: float32 [1536], P('gy'), may hold values from 0.3 to 3
Outputs:
- derivs: float32 [3, 8, 1536, 8192], P(None, None, 'gy', 'gx')
- vorticity: float32 [8, 1536, 8192], P(None, 'gy', 'gx')
All inputs are finite; a program needn't handle non-finite values.
Results may differ from a plain program's by a relative error of at most 0.00007.
Values sent between devices are 32-bit elements; how exact they have to be, the bound alone decides.
A program may use at most 64 MiB of HBM per device.

v0:
```python
import jax
import jax.numpy as jnp
from jax import lax
from jax.sharding import PartitionSpec as P

coupling = 1.0 / 3.0
near_weight = 7.0 / 9.0
far_weight = 1.0 / 36.0


def padded_2(block, sides, width):
    for axis, dim in sides:
        count = lax.axis_size(axis)
        forward = [(i, i + 1) for i in range(count - 1)]
        forward.append((count - 1, 0))
        backward = [(target, source) for source, target in forward]
        low = lax.ppermute(
            lax.slice_in_dim(block, block.shape[dim] - width, None, axis=dim), axis, forward
        )
        high = lax.ppermute(lax.slice_in_dim(block, 0, width, axis=dim), axis, backward)
        block = jnp.concatenate([low, block, high], axis=dim)
    return block


def band_inverse(length):
    index = jnp.arange(length)
    lower_diag = jnp.where(index > 0, coupling, 0.0).astype(jnp.float32)
    upper_diag = jnp.where(index < length - 1, coupling, 0.0).astype(jnp.float32)
    main_diag = jnp.ones((length,), jnp.float32)
    identity = jnp.eye(length, dtype=jnp.float32)
    return lax.linalg.tridiagonal_solve(lower_diag, main_diag, upper_diag, identity)


def per_device(velocity, metric_x, metric_y):
    points = velocity.shape[3]
    line_count = velocity.shape[0] * velocity.shape[1] * velocity.shape[2]
    rim = 2
    padded = padded_2(velocity, (("gx", 3),), rim)
    extent = points + 2 * rim - 4
    right_side = near_weight * (
        padded[..., 3 : extent + 3] - padded[..., 1 : extent + 1]
    ) + far_weight * (padded[..., 4 : extent + 4] - padded[..., 0:extent])
    flat = right_side.reshape((line_count, extent))
    inverse = band_inverse(points)
    particular = jnp.dot(flat, jnp.transpose(inverse), precision=lax.Precision.HIGHEST)
    left_column = inverse[:, 0]
    right_column = inverse[:, points - 1]
    corner_first = inverse[0, 0]
    corner_last = inverse[points - 1, points - 1]
    ends = jnp.stack([particular[:, 0], particular[:, points - 1]])
    extended = padded_2(ends, (("gx", 0),), 1)
    denominator = 1.0 - coupling * coupling * corner_first * corner_last
    prev_end = extended[0]
    next_start = extended[3]
    prev_last = (prev_end - coupling * corner_last * ends[0]) / denominator
    next_first = (next_start - coupling * corner_first * ends[1]) / denominator
    slope = (
        particular
        - coupling * prev_last[:, None] * left_column[None, :]
        - coupling * next_first[:, None] * right_column[None, :]
    )
    derivs = slope.reshape(velocity.shape) * metric_x[None, None, None, :]
    upart = padded_2(velocity[0], (("gy", 1),), 3)
    rows_y = velocity.shape[2]
    shear = (
        45.0 * (upart[:, 4 : rows_y + 4] - upart[:, 2 : rows_y + 2])
        - 9.0 * (upart[:, 5 : rows_y + 5] - upart[:, 1 : rows_y + 1])
        + (upart[:, 6 : rows_y + 6] - upart[:, 0:rows_y])
    ) / 60.0
    vorticity = derivs[1] - metric_y[None, :, None] * shear
    return (derivs, vorticity)


def solution(mesh):
    in_specs = (P(None, None, "gy", "gx"), P("gx"), P("gy"))
    out_specs = (P(None, None, "gy", "gx"), P(None, "gy", "gx"))
    return jax.shard_map(
        per_device, mesh=mesh, in_specs=in_specs, out_specs=out_specs, check_vma=False
    )
```

profile of v0, /device:TPU:1, one launch (start us, length us, event | category | flops | bytes accessed | tf_op | source)
XLA Modules:
  0.0 757.7 jit_solution(13235260253506243324)
XLA Ops:
  0.6 4.6 fusion.29
  5.3 2.6 copy.15
  7.8 8.6 %collective-permute-start = (f32[3,8,192,2]{2,1,3,0:T(8,128)S(1)}, f32[3,8,192,2]{2,1,3,0:T(8,128)S(1)}, u32[]{:S(2)}, u32[]{:S(2)}) collective-permute-start(f32[3,8,192,2]{2,1,3,0:T(8,128)S(1)} %copy.15), channel_id=1, source_target_pairs={{8,0},{16,8},{24,16},{32,24},{40,32},{48,40},{56,48},{64,56},{72,6... | collective-permute-start | bytes 110600 | tf_op jit(solution)/shard_map/ppermute | solution.py:20
  16.5 0.9 copy.16
  17.5 1.6 slice_bitcast_fusion.1
  19.0 1.1 copy-done.1
  20.2 1.0 collective-permute-start.4
  21.2 1.2 collective-permute-start.5
  23.3 0.7 fusion.36
  24.0 0.7 fusion.37
  25.6 455.1 %while.32 = (s32[]{:T(128)}, f32[]{:T(128)}, f32[256]{0:T(256)S(1)}, f32[7,32]{1,0:T(8,128)S(1)}, f32[7,32,256]{2,1,0:T(8,128)S(1)}, /*index=5*/f32[7,32]{1,0:T(...) while((s32[]{:T(128)}, f32[]{:T(128)}, ...), condition=%wide.region_1.2_spmd, body=%wide.region_0.1_spmd.sunk | while | flops 24705 | bytes 269033 | solution.py:31
  25.7 0.7 fusion.53
  27.5 0.7 fusion.52
  68.8 19.8 %subtract_divide_fusion.125 = (f32[256]{0:T(256)S(1)}, f32[256]{0:T(256)S(1)}, f32[256]{0:T(256)S(1)}, f32[256]{0:T(256)S(1)}, f32[256]{0:T(256)S(1)}, /*index=5...) fusion(f32[256]{0:T(256)S(1)} %bitcast.1138, ...), kind=kLoop, calls=%fused_computation.35.clone.1 | loop fusion | flops 24576 | bytes 66816 | tf_op jit(solution)/shard_map/while/body/eval_jaxpr/div | solution.py:31
  88.8 0.7 concatenate.54
  90.7 0.7 fusion.53
  92.5 0.7 fusion.52
  133.8 19.8 %subtract_divide_fusion.125 = (f32[256]{0:T(256)S(1)}, f32[256]{0:T(256)S(1)}, f32[256]{0:T(256)S(1)}, f32[256]{0:T(256)S(1)}, f32[256]{0:T(256)S(1)}, /*index=5...) fusion(f32[256]{0:T(256)S(1)} %bitcast.1138, ...), kind=kLoop, calls=%fused_computation.35.clone.1 | loop fusion | flops 24576 | bytes 66816 | tf_op jit(solution)/shard_map/while/body/eval_jaxpr/div | solution.py:31
  153.8 0.7 concatenate.54
  155.7 0.7 fusion.53
  157.5 0.7 fusion.52
  198.8 19.8 %subtract_divide_fusion.125 = (f32[256]{0:T(256)S(1)}, f32[256]{0:T(256)S(1)}, f32[256]{0:T(256)S(1)}, f32[256]{0:T(256)S(1)}, f32[256]{0:T(256)S(1)}, /*index=5...) fusion(f32[256]{0:T(256)S(1)} %bitcast.1138, ...), kind=kLoop, calls=%fused_computation.35.clone.1 | loop fusion | flops 24576 | bytes 66816 | tf_op jit(solution)/shard_map/while/body/eval_jaxpr/div | solution.py:31
  218.8 0.7 concatenate.54
  220.7 0.7 fusion.53
  222.6 0.7 fusion.52
  263.8 19.8 %subtract_divide_fusion.125 = (f32[256]{0:T(256)S(1)}, f32[256]{0:T(256)S(1)}, f32[256]{0:T(256)S(1)}, f32[256]{0:T(256)S(1)}, f32[256]{0:T(256)S(1)}, /*index=5...) fusion(f32[256]{0:T(256)S(1)} %bitcast.1138, ...), kind=kLoop, calls=%fused_computation.35.clone.1 | loop fusion | flops 24576 | bytes 66816 | tf_op jit(solution)/shard_map/while/body/eval_jaxpr/div | solution.py:31
  283.8 0.7 concatenate.54
  285.7 0.7 fusion.53
  287.6 0.7 fusion.52
  328.8 19.8 %subtract_divide_fusion.125 = (f32[256]{0:T(256)S(1)}, f32[256]{0:T(256)S(1)}, f32[256]{0:T(256)S(1)}, f32[256]{0:T(256)S(1)}, f32[256]{0:T(256)S(1)}, /*index=5...) fusion(f32[256]{0:T(256)S(1)} %bitcast.1138, ...), kind=kLoop, calls=%fused_computation.35.clone.1 | loop fusion | flops 24576 | bytes 66816 | tf_op jit(solution)/shard_map/while/body/eval_jaxpr/div | solution.py:31
  350.7 0.7 fusion.53
  352.6 0.7 fusion.52
  393.9 19.8 %subtract_divide_fusion.125 = (f32[256]{0:T(256)S(1)}, f32[256]{0:T(256)S(1)}, f32[256]{0:T(256)S(1)}, f32[256]{0:T(256)S(1)}, f32[256]{0:T(256)S(1)}, /*index=5...) fusion(f32[256]{0:T(256)S(1)} %bitcast.1138, ...), kind=kLoop, calls=%fused_computation.35.clone.1 | loop fusion | flops 24576 | bytes 66816 | tf_op jit(solution)/shard_map/while/body/eval_jaxpr/div | solution.py:31
  413.8 0.7 concatenate.54
  415.7 0.7 fusion.53
  417.6 0.7 fusion.52
  458.9 19.8 %subtract_divide_fusion.125 = (f32[256]{0:T(256)S(1)}, f32[256]{0:T(256)S(1)}, f32[256]{0:T(256)S(1)}, f32[256]{0:T(256)S(1)}, f32[256]{0:T(256)S(1)}, /*index=5...) fusion(f32[256]{0:T(256)S(1)} %bitcast.1138, ...), kind=kLoop, calls=%fused_computation.35.clone.1 | loop fusion | flops 24576 | bytes 66816 | tf_op jit(solution)/shard_map/while/body/eval_jaxpr/div | solution.py:31
  480.8 0.7 fusion.35
  521.9 19.3 %subtract_divide_fusion.32 = (f32[256]{0:T(256)S(1)}, f32[256]{0:T(256)S(1)}, f32[256]{0:T(256)S(1)}, f32[256]{0:T(256)S(1)}, f32[256]{0:T(256)S(1)}, /*index=5*...) fusion(f32[256]{0:T(256)S(1)} %bitcast.1326, ...), kind=kLoop, calls=%fused_computation.218 | loop fusion | flops 23808 | bytes 64760 | tf_op jit(solution)/shard_map/eval_jaxpr/div | solution.py:31
  541.4 152.3 %while.33 = (s32[]{:T(128)}, f32[256]{0:T(256)S(1)}, f32[7,32,256]{2,1,0:T(8,128)S(1)}, f32[7,32,256]{2,1,0:T(8,128)S(1)}, f32[7,32]{1,0:T(8,128)S(1)}, /*index=...) while((s32[]{:T(128)}, f32[256]{0:T(256)S(1)}, ...), condition=%wide.region_3.4_spmd, body=%wide.region_2.3_spmd.sunk | while | flops 16418 | bytes 266713 | solution.py:31
  541.4 0.7 fusion.55
  543.0 20.0 %multiply_subtract_fusion.126 = (f32[256]{0:T(256)S(1)}, f32[256]{0:T(256)S(1)}, f32[256]{0:T(256)S(1)}, f32[256]{0:T(256)S(1)}, f32[256]{0:T(256)S(1)}, /*index...) fusion(f32[256]{0:T(256)S(1)} %bitcast.1187, ...), kind=kLoop, calls=%fused_computation.101.clone.1 | loop fusion | flops 16384 | bytes 66688 | tf_op jit(solution)/shard_map/while/body/eval_jaxpr/sub | solution.py:31
  563.1 0.7 fusion.55
  564.8 20.0 %multiply_subtract_fusion.126 = (f32[256]{0:T(256)S(1)}, f32[256]{0:T(256)S(1)}, f32[256]{0:T(256)S(1)}, f32[256]{0:T(256)S(1)}, f32[256]{0:T(256)S(1)}, /*index...) fusion(f32[256]{0:T(256)S(1)} %bitcast.1187, ...), kind=kLoop, calls=%fused_computation.101.clone.1 | loop fusion | flops 16384 | bytes 66688 | tf_op jit(solution)/shard_map/while/body/eval_jaxpr/sub | solution.py:31
  584.9 0.7 fusion.55
  586.5 20.0 %multiply_subtract_fusion.126 = (f32[256]{0:T(256)S(1)}, f32[256]{0:T(256)S(1)}, f32[256]{0:T(256)S(1)}, f32[256]{0:T(256)S(1)}, f32[256]{0:T(256)S(1)}, /*index...) fusion(f32[256]{0:T(256)S(1)} %bitcast.1187, ...), kind=kLoop, calls=%fused_computation.101.clone.1 | loop fusion | flops 16384 | bytes 66688 | tf_op jit(solution)/shard_map/while/body/eval_jaxpr/sub | solution.py:31
  606.7 0.7 fusion.55
  608.3 20.0 %multiply_subtract_fusion.126 = (f32[256]{0:T(256)S(1)}, f32[256]{0:T(256)S(1)}, f32[256]{0:T(256)S(1)}, f32[256]{0:T(256)S(1)}, f32[256]{0:T(256)S(1)}, /*index...) fusion(f32[256]{0:T(256)S(1)} %bitcast.1187, ...), kind=kLoop, calls=%fused_computation.101.clone.1 | loop fusion | flops 16384 | bytes 66688 | tf_op jit(solution)/shard_map/while/body/eval_jaxpr/sub | solution.py:31
  628.4 0.7 fusion.55
  630.0 20.0 %multiply_subtract_fusion.126 = (f32[256]{0:T(256)S(1)}, f32[256]{0:T(256)S(1)}, f32[256]{0:T(256)S(1)}, f32[256]{0:T(256)S(1)}, f32[256]{0:T(256)S(1)}, /*index...) fusion(f32[256]{0:T(256)S(1)} %bitcast.1187, ...), kind=kLoop, calls=%fused_computation.101.clone.1 | loop fusion | flops 16384 | bytes 66688 | tf_op jit(solution)/shard_map/while/body/eval_jaxpr/sub | solution.py:31
  650.2 0.7 fusion.55
  651.8 20.0 %multiply_subtract_fusion.126 = (f32[256]{0:T(256)S(1)}, f32[256]{0:T(256)S(1)}, f32[256]{0:T(256)S(1)}, f32[256]{0:T(256)S(1)}, f32[256]{0:T(256)S(1)}, /*index...) fusion(f32[256]{0:T(256)S(1)} %bitcast.1187, ...), kind=kLoop, calls=%fused_computation.101.clone.1 | loop fusion | flops 16384 | bytes 66688 | tf_op jit(solution)/shard_map/while/body/eval_jaxpr/sub | solution.py:31
  671.9 0.7 fusion.55
  673.6 20.0 %multiply_subtract_fusion.126 = (f32[256]{0:T(256)S(1)}, f32[256]{0:T(256)S(1)}, f32[256]{0:T(256)S(1)}, f32[256]{0:T(256)S(1)}, f32[256]{0:T(256)S(1)}, /*index...) fusion(f32[256]{0:T(256)S(1)} %bitcast.1187, ...), kind=kLoop, calls=%fused_computation.101.clone.1 | loop fusion | flops 16384 | bytes 66688 | tf_op jit(solution)/shard_map/while/body/eval_jaxpr/sub | solution.py:31
  693.6 19.4 %multiply_subtract_fusion.33 = (f32[256]{0:T(256)S(1)}, f32[256]{0:T(256)S(1)}, f32[256]{0:T(256)S(1)}, f32[256]{0:T(256)S(1)}, f32[256]{0:T(256)S(1)}, /*index=...) fusion(f32[256]{0:T(256)S(1)} %bitcast.1314, ...), kind=kLoop, calls=%fused_computation.187 | loop fusion | flops 15872 | bytes 64636 | tf_op jit(solution)/shard_map/eval_jaxpr/sub | solution.py:31
  713.2 0.8 copy.11
  714.0 2.2 copy.13
  716.1 12.5 %fusion.3 = f32[3,8,192,256]{3,2,1,0:T(8,128)S(1)} fusion(f32[3,8,192,2]{3,2,1,0:T(8,128)} %copy.13, f32[3,8,192,256]{3,2,1,0:T(8,128)} %param.7, f32[3,8,192,2]{3,2,1,0:T(8,128)S(1)} %copy.11), kind=kLoop, calls=%fused_computation.140 | loop fusion | flops 10616832 | bytes 9510912 | tf_op jit(solution)/shard_map/add | solution.py:40
  728.6 4.8 fusion.41
  733.5 5.1 collective-permute-start.3
  742.9 3.1 multiply_subtract_fusion.32
  745.9 6.1 copy.14
  752.0 3.0 broadcast_multiply_fusion
  755.1 2.6 fusion.13
  (163 shorter events, 26.4 us)
Async XLA Ops:
  7.8 705.4 %collective-permute-start = (f32[3,8,192,2]{2,1,3,0:T(8,128)S(1)}, f32[3,8,192,2]{2,1,3,0:T(8,128)S(1)}, u32[]{:S(2)}, u32[]{:S(2)}) collective-permute-start(f32[3,8,192,2]{2,1,3,0:T(8,128)S(1)} %copy.15), channel_id=1, source_target_pairs={{8,0},{16,8},{24,16},{32,24},{40,32},{48,40},{56,48},{64,56},{72,6... | collective-permute-start | bytes 110600 | tf_op jit(solution)/shard_map/ppermute | solution.py:20
  17.4 696.6 %collective-permute-start.1 = (f32[3,8,192,2]{2,1,3,0:T(8,128)S(1)}, f32[3,8,192,2]{2,1,3,0:T(8,128)S(1)}, u32[]{:S(2)}, u32[]{:S(2)}) collective-permute-start(f32[3,8,192,2]{2,1,3,0:T(8,128)S(1)} %copy.16), channel_id=1, source_target_pairs={{0,8},{8,16},{16,24},{24,32},{32,40},{40,48},{48,56},{56,64},{64,7... | collective-permute-start | bytes 110600 | tf_op jit(solution)/shard_map/ppermute | solution.py:17
  19.0 1.1 copy-start.1
  20.2 734.9 %collective-permute-start.4 = (f32[8,3,256]{2,1,0:T(4,128)S(1)}, f32[8,3,256]{2,1,0:T(4,128)S(1)}, u32[]{:S(2)}, u32[]{:S(2)}) collective-permute-start(f32[8,3,256]{2,1,0:T(4,128)S(1)} %get-tuple-element.479), channel_id=1, source_target_pairs={{1,0},{2,1},{3,2},{4,3},{5,4},{6,5},{7,6},{0,7},{9,8},{10,9},{11,1... | collective-permute-start | bytes 73736 | tf_op jit(solution)/shard_map/ppermute | solution.py:20
  21.2 733.9 %collective-permute-start.5 = (f32[8,3,256]{2,1,0:T(4,128)S(1)}, f32[8,3,256]{2,1,0:T(4,128)S(1)}, u32[]{:S(2)}, u32[]{:S(2)}) collective-permute-start(f32[8,3,256]{2,1,0:T(4,128)S(1)} %get-tuple-element.480), channel_id=1, source_target_pairs={{0,1},{1,2},{2,3},{3,4},{4,5},{5,6},{6,7},{7,0},{8,9},{9,10},{10,1... | collective-permute-start | bytes 73736 | tf_op jit(solution)/shard_map/ppermute | solution.py:17
  480.7 232.3 %copy-start.4 = (f32[192]{0:T(256)S(1)}, f32[192]{0:T(256)}, u32[]{:S(2)}) copy-start(f32[192]{0:T(256)} %param.9) | copy-start | bytes 2308
  733.4 9.3 %collective-permute-start.2 = (f32[1,4608]{1,0:T(1,128)S(1)}, f32[1,4608]{1,0:T(1,128)S(1)}, u32[]{:S(2)}, u32[]{:S(2)}) collective-permute-start(f32[1,4608]{1,0:T(1,128)S(1)} %get-tuple-element.476), channel_id=1, source_target_pairs={{0,8},{8,16},{16,24},{24,32},{32,40},{40,48},{48,56},{56,64},{64,7... | collective-permute-start | bytes 55304 | tf_op jit(solution)/shard_map/ppermute | solution.py:17
  733.5 9.2 %collective-permute-start.3 = (f32[1,4608]{1,0:T(1,128)S(1)}, f32[1,4608]{1,0:T(1,128)S(1)}, u32[]{:S(2)}, u32[]{:S(2)}) collective-permute-start(f32[1,4608]{1,0:T(1,128)S(1)} %get-tuple-element.475), channel_id=1, source_target_pairs={{8,0},{16,8},{24,16},{32,24},{40,32},{48,40},{56,48},{64,56},{72,6... | collective-permute-start | bytes 55304 | tf_op jit(solution)/shard_map/ppermute | solution.py:20
  745.9 6.1 copy-start.3
  752.0 3.0 copy-start.2
  755.0 2.7 copy-start
where the time goes:
time: 767 us; the launch traced here: 758 us
  other arithmetic  339 us (44%)
  loops' own time  289 us (38%)
  local copies, waits for them, and re-layouts  67 us (9%)
  between operations  42.3 us (6%)
  starting transfers between devices  16.1 us (2%)
    another operation x2, loops' own time, band_inverse(): lax.linalg.tridiagonal_solve(lower_diag, main_diag, upper_diag, identity)  289 us
    sub x8, other arithmetic, band_inverse(): lax.linalg.tridiagonal_solve(lower_diag, main_diag, upper_diag, identity)  159 us
    div x8, other arithmetic, band_inverse(): lax.linalg.tridiagonal_solve(lower_diag, main_diag, upper_diag, identity)  158 us
    slice x85, local copies, waits for them, and re-layouts, band_inverse(): lax.linalg.tridiagonal_solve(lower_diag, main_diag, upper_diag, identity)  37.5 us
  transfers between devices with their start and end apart: 6, of which 0 were waited for; matrix products, arithmetic and copies ran while one was open for 53% of the time, Pallas kernels for 0%

commit v1 on v0

v1 whole, which is shorter than its diff:
```python
import numpy as np
import jax
import jax.numpy as jnp
from jax import lax
from jax.experimental import pallas as pl
from jax.experimental.pallas import tpu as pltpu
from jax.sharding import PartitionSpec as P

ratio = (np.sqrt(5.0) - 3.0) / 2.0
green = 1.0 / (1.0 + 2.0 * ratio / 3.0)
tail = green * 25.0 / 36.0
centre = green * (7.0 / 9.0 + ratio / 18.0)
MESH = pl.DeviceIdType.MESH
f32 = jnp.float32
bf16 = jnp.bfloat16


def powers_of_ratio(exponent, bits):
    value = jnp.ones(exponent.shape, f32)
    for bit in range(bits):
        factor = float(ratio ** (2**bit))
        factor = factor if abs(factor) > 1e-37 else 0.0
        value = value * jnp.where((exponent >> bit) & 1 == 1, factor, 1.0)
    return value


def band_matrix(points):
    source = lax.broadcasted_iota(jnp.int32, (points, points), 0)
    target = lax.broadcasted_iota(jnp.int32, (points, points), 1)
    distance = jnp.abs(target - source - 1)
    values = jnp.where(distance == 0, centre, tail * powers_of_ratio(distance, 9))
    values = jnp.where(source < points - 2, values, 0.0)
    high = values.astype(bf16)
    return high, (values - high.astype(f32)).astype(bf16)


def ring(axis):
    count = lax.axis_size(axis)
    me = lax.axis_index(axis)
    return lax.rem(me + 1, count), lax.rem(me + count - 1, count)


def local_kernel(
    velocity, metric_y, local, sheared, lefts, rights,
    my_line, band, u_rows, others, own, sent, from_left, from_right,
    my_sem, in_sem, y_send, y_recv, x_send, x_recv,
):
    fields, depth, rows, points = velocity.shape
    half = points // 2
    groups = rows // 64
    right, left = ring("gx")
    above, below = ring("gy")

    barrier = pltpu.get_barrier_semaphore()
    for axis, place in (("gx", right), ("gx", left), ("gy", above), ("gy", below)):
        pl.semaphore_signal(barrier, inc=1, device_id={axis: place}, device_id_type=MESH)

    loads = []
    for field in range(fields):
        if field == 0:
            target = u_rows.at[:, 8 : rows + 8]
        else:
            target = others.at[field - 1]
        load = pltpu.make_async_copy(velocity.at[field], target, in_sem.at[field])
        load.start()
        loads.append(load)

    my_load = pltpu.make_async_copy(metric_y, my_line, my_sem)
    my_load.start()
    band[0], band[1] = band_matrix(points)

    pl.semaphore_wait(barrier, 4)
    y_copies = [
        pltpu.make_async_remote_copy(
            velocity.at[0, :, rows - 8 : rows], u_rows.at[:, 0:8],
            y_send.at[0], y_recv.at[0], device_id={"gy": above}, device_id_type=MESH,
        ),
        pltpu.make_async_remote_copy(
            velocity.at[0, :, 0:8], u_rows.at[:, rows + 8 : rows + 16],
            y_send.at[1], y_recv.at[1], device_id={"gy": below}, device_id_type=MESH,
        ),
    ]
    for copy in y_copies:
        copy.start()

    lane = lax.broadcasted_iota(jnp.int32, (rows, half), 1)
    row = lax.broadcasted_iota(jnp.int32, (rows, half), 0)
    odd = lax.rem(lane, 2)
    slot = lane // 2 - lax.rem(row // 8, 8)
    small_odd = lax.broadcasted_iota(jnp.int32, (groups, 8, half), 2) % 2 == 1

    def lanes(x, shift):
        return pltpu.roll(x, shift % half, 2)

    x_copies = []
    for field in range(fields):
        loads[field].wait()

        def plane(z, packs):
            if field == 0:
                block = u_rows[z, 8 : rows + 8, :]
            else:
                block = others[field - 1, z]
            step = pltpu.roll(block, points - 2, 1) - block
            high = step.astype(bf16)
            low = (step - high.astype(f32)).astype(bf16)
            result = (
                jnp.dot(high, band[0], preferred_element_type=f32)
                + jnp.dot(low, band[0], preferred_element_type=f32)
                + jnp.dot(high, band[1], preferred_element_type=f32)
            )
            local[field, z] = result
            here = slot == z * 8

            def packed(values):
                return jnp.where(here, values, 0.0).reshape(groups, 8, 8, half).sum(axis=1)

            parts = (
                packed(jnp.take_along_axis(block[:, :half], 1 - odd, axis=1)),
                packed(jnp.take_along_axis(block[:, half:], half - 2 + odd, axis=1)),
                packed(jnp.broadcast_to(result[:, :1], (rows, half))),
                packed(jnp.broadcast_to(result[:, points - 1 :], (rows, half))),
            )
            return tuple(a + b for a, b in zip(packs, parts))

        zero = jnp.zeros((groups, 8, half), f32)
        first, last, start, end = lax.fori_loop(0, depth, plane, (zero,) * 4)
        own[0, field] = first
        own[1, field] = last
        sent[0, field] = jnp.where(
            small_odd, first, ratio * start + (tail * ratio) * (first - lanes(first, -1))
        )
        sent[1, field] = jnp.where(
            small_odd, last, ratio * end + (tail * ratio) * (lanes(last, -1) - last)
        )
        for side, place, target in ((0, left, from_right), (1, right, from_left)):
            copy = pltpu.make_async_remote_copy(
                sent.at[side, field], target.at[field],
                x_send.at[side, field], x_recv.at[side, field],
                device_id={"gx": place}, device_id_type=MESH,
            )
            copy.start()
            x_copies.append(copy)

    for copy in y_copies:
        copy.wait()
    square = (
        lax.broadcasted_iota(jnp.int32, (rows, rows), 0)
        == lax.broadcasted_iota(jnp.int32, (rows, rows), 1)
    )
    my_load.wait()
    my_row = my_line[...].reshape(1, rows)
    my_column = jnp.sum(jnp.where(square, my_row, 0.0), axis=1, keepdims=True)
    my_full = jnp.broadcast_to(my_column / 60.0, (rows, points))

    def shear_plane(z, carry):
        def shifted(k):
            return u_rows[z, 8 + k : rows + 8 + k, :]

        sheared[z] = my_full * (
            45.0 * (shifted(1) - shifted(-1))
            - 9.0 * (shifted(2) - shifted(-2))
            + (shifted(3) - shifted(-3))
        )
        return carry

    lax.fori_loop(0, depth, shear_plane, 0)

    for copy in x_copies:
        copy.wait()
    for field in range(fields):
        near = own[0, field]
        far = from_left[field]
        far_edge = lanes(far, -1)
        straddle = near - far_edge
        total = far + tail * straddle + (tail * ratio) * (lanes(near, -1) - far_edge)
        lefts[field] = jnp.where(
            small_odd, lanes(total + (centre - tail) * straddle, 1), total
        )
        near = own[1, field]
        far = from_right[field]
        far_edge = lanes(far, -1)
        straddle = far_edge - near
        total = far + tail * straddle + (tail * ratio) * (far_edge - lanes(near, -1))
        rights[field] = jnp.where(
            small_odd, lanes(total + (centre - tail) * straddle, 1), total
        )


def finish_kernel(local, sheared, lefts, rights, metric_x, derivs, vorticity, staged, out_sem):
    fields, depth, rows, points = derivs.shape
    half = points // 2
    groups = rows // 64
    lane = lax.broadcasted_iota(jnp.int32, (rows, half), 1)
    row = lax.broadcasted_iota(jnp.int32, (rows, half), 0)
    slot = 2 * lax.rem(row // 8, 8)
    left_slot = slot + jnp.where(lane == 0, 1, 0)
    right_slot = slot + jnp.where(lane == half - 1, 1, 0)
    mx = metric_x[...].reshape(1, points)
    column = lax.broadcasted_iota(jnp.int32, (1, half), 1)
    left_powers = powers_of_ratio(column, 7)
    right_powers = powers_of_ratio(half - 1 - column, 7)

    def spread(pack, index):
        wide = jnp.broadcast_to(pack[:, None], (groups, 8, 8, half)).reshape(rows, half)
        return jnp.take_along_axis(wide, index, axis=1)

    def copies(z):
        out = [
            pltpu.make_async_copy(staged.at[field, z], derivs.at[field, z], out_sem.at[field, z])
            for field in range(fields)
        ]
        out.append(pltpu.make_async_copy(staged.at[fields, z], vorticity.at[z], out_sem.at[fields, z]))
        return out

    def plane(z, carry):
        sends = copies(z)
        for field in range(fields):
            block = local[field, z]
            low = block[:, :half] + spread(lefts[field], left_slot + 16 * z) * left_powers
            high = block[:, half:] + spread(rights[field], right_slot + 16 * z) * right_powers
            low = low * mx[:, :half]
            high = high * mx[:, half:]
            staged[field, z, :, :half] = low
            staged[field, z, :, half:] = high
            sends[field].start()
            if field == 1:
                staged[fields, z, :, :half] = low - sheared[z, :, :half]
                staged[fields, z, :, half:] = high - sheared[z, :, half:]
                sends[fields].start()
        return carry

    lax.fori_loop(0, depth, plane, 0)

    def drain(z, carry):
        for copy in copies(z):
            copy.wait()
        return carry

    lax.fori_loop(0, depth, drain, 0)


def per_device(velocity, metric_x, metric_y):
    fields, depth, rows, points = velocity.shape
    half = points // 2
    groups = rows // 64
    packs = (fields, groups, 8, half)
    anywhere = pl.BlockSpec(memory_space=pl.ANY)
    hbm = pl.BlockSpec(memory_space=pltpu.HBM)
    vmem = pl.BlockSpec(memory_space=pltpu.VMEM)
    local, sheared, lefts, rights = pl.pallas_call(
        local_kernel,
        out_shape=(
            OUT((fields, depth, rows, points), f32),
            OUT((depth, rows, points), f32),
            OUT(packs, f32),
            OUT(packs, f32),
        ),
        in_specs=[hbm, hbm],
        out_specs=(vmem,) * 4,
        scratch_shapes=[
            pltpu.VMEM((rows,), f32),
            pltpu.VMEM((2, points, points), bf16),
            pltpu.VMEM((depth, rows + 16, points), f32),
            pltpu.VMEM((fields - 1, depth, rows, points), f32),
            pltpu.VMEM((2,) + packs, f32),
            pltpu.VMEM((2,) + packs, f32),
            pltpu.VMEM(packs, f32),
            pltpu.VMEM(packs, f32),
            pltpu.SemaphoreType.DMA(()),
            pltpu.SemaphoreType.DMA((fields,)),
            pltpu.SemaphoreType.DMA((2,)),
            pltpu.SemaphoreType.DMA((2,)),
            pltpu.SemaphoreType.DMA((2, fields)),
            pltpu.SemaphoreType.DMA((2, fields)),
        ],
        compiler_params=pltpu.CompilerParams(
            collective_id=0, has_side_effects=True, vmem_limit_bytes=24 * 1024 * 1024
        ),
        name="local",
    )(
        pltpu.with_memory_space_constraint(velocity, pltpu.HBM),
        pltpu.with_memory_space_constraint(metric_y, pltpu.HBM),
    )
    return pl.pallas_call(
        finish_kernel,
        out_shape=(
            jax.ShapeDtypeStruct((fields, depth, rows, points), f32),
            jax.ShapeDtypeStruct((depth, rows, points), f32),
        ),
        in_specs=[vmem] * 5,
        out_specs=(anywhere, anywhere),
        scratch_shapes=[
            pltpu.VMEM((fields + 1, depth, rows, points), f32),
            pltpu.SemaphoreType.DMA((fields + 1, depth)),
        ],
        compiler_params=pltpu.CompilerParams(vmem_limit_bytes=24 * 1024 * 1024),
        name="finish",
    )(local, sheared, lefts, rights, metric_x)


OUT = pltpu.VMEM


def solution(mesh):
    in_specs = (P(None, None, "gy", "gx"), P("gx"), P("gy"))
    out_specs = (P(None, None, "gy", "gx"), P(None, "gy", "gx"))
    return jax.shard_map(
        per_device, mesh=mesh, in_specs=in_specs, out_specs=out_specs, check_vma=False
    )
```

time: 767 us -> 27.5 us (0.04); the launches traced: 758 us -> 27.4 us
  other arithmetic: 339 us -> 0 us
  loops' own time: 289 us -> 0 us
  local copies, waits for them, and re-layouts: 67 us -> 0.01 us
  between operations: 42.3 us -> 0.65 us
  Pallas kernels: 0 us -> 26.8 us
  starting transfers between devices: 16.1 us -> 0 us
    another operation x2 -> x0, loops' own time: 289 us -> none  [band_inverse(): lax.linalg.tridiagonal_solve(lower_diag, main_diag, upper_diag, identity)]
    sub x10 -> x0, other arithmetic: 165 us -> none  [the longest x8 159 us: band_inverse(): lax.linalg.tridiagonal_solve(lower_diag, main_diag, upper_diag, identity)]
    div x8 -> x0, other arithmetic: 158 us -> none  [band_inverse(): lax.linalg.tridiagonal_solve(lower_diag, main_diag, upper_diag, identity)]
    slice x90 -> x0, local copies, waits for them, and re-layouts: 43.5 us -> none  [the longest x85 37.5 us: band_inverse(): lax.linalg.tridiagonal_solve(lower_diag, main_diag, upper_diag, identity)]
    pallas_call x0 -> x2, Pallas kernels: none -> 26.8 us  [the longest x1 21.9 us: per_device(): pl.pallas_call(local_kernel, out_shape=(OUT((fields, depth, rows, points)...]
    ppermute x6 -> x0, starting transfers between devices: 16.1 us -> none  [the longest x3 14.7 us: padded_2(): lax.ppermute(lax.slice_in_dim(block, 0, width, axis=dim), axis, backward)]
    add x1 -> x0, other arithmetic: 12.5 us -> none  [per_device(): near_weight * (padded[..., 3:extent + 3] - padded[..., 1:extent + 1])]
  transfers between devices with their start and end apart: 6 -> 0, of which waited for: 0 -> 0; matrix products, arithmetic and copies ran while one was open for 53% -> 0% of each run, Pallas kernels for 0% -> 0%
where the time goes in v1:
time: 27.5 us; the launch traced here: 27.4 us
  Pallas kernels  26.8 us (97%)
  between operations  0.65 us (2%)
    pallas_call x1, Pallas kernels, per_device(): pl.pallas_call(local_kernel, out_shape=(OUT((fields, depth, rows, points)...  21.9 us
    pallas_call x1, Pallas kernels, per_device(): pl.pallas_call(finish_kernel, out_shape=(jax.ShapeDtypeStruct((fields, de...  4.92 us

profile of v1, /device:TPU:1, one launch (start us, length us, event | category | flops | bytes accessed | tf_op | source)
XLA Modules:
  0.0 27.4 jit_solution(7640754886105780003)
XLA Ops:
  0.6 0.0 copy-start
  0.6 21.9 %local.1 = (f32[3,8,192,256]{3,2,1,0:T(8,128)S(1)}, f32[8,192,256]{2,1,0:T(8,128)S(1)}, f32[3,3,8,128]{3,2,1,0:T(8,128)S(1)}, f32[3,3,8,128]{3,2,1,0:T(8,128)S(1)}) custom-call(f32[3,8,192,256]{3,2,1,0:T(8,128)} %velocity.1, f32[192]{0:T(256)} %metric_y.1), custom_call_target="tpu_custom_call" | custom-call | tf_op jit(solution)/shard_map/local/pallas_call | solution.py:251
  22.5 0.0 copy-done
  22.5 4.9 %finish.1 = (f32[3,8,192,256]{3,2,1,0:T(8,128)}, f32[8,192,256]{2,1,0:T(8,128)}) custom-call(f32[3,8,192,256]{3,2,1,0:T(8,128)S(1)} %get-tuple-element.6.local, f32[8,192,256]{2,1,0:T(8,128)S(1)} %get-tuple-element.7.sheared, f32[3,3,8,128]{3,2,1,0:T(8,128)S(1)} %get-tuple-element.8.lefts, f32[3,3,8,128]{3,2,1,0:T(8,128)S(1)} %get-tuple-element.9.rights, ...), custom_call_target="tpu_custom_call" | custom-call | tf_op jit(solution)/shard_map/finish/pallas_call | solution.py:285
Async XLA Ops:
  0.6 21.9 %copy-start = (f32[256]{0:T(256)S(1)}, f32[256]{0:T(256)}, u32[]{:S(2)}) copy-start(f32[256]{0:T(256)} %metric_x.1) | copy-start | bytes 3076

commit v2 on v1

v2 whole, which is shorter than its diff:
```python
import numpy as np
import jax
import jax.numpy as jnp
from jax import lax
from jax.experimental import pallas as pl
from jax.experimental.pallas import tpu as pltpu
from jax.sharding import PartitionSpec as P

ratio = (np.sqrt(5.0) - 3.0) / 2.0
green = 1.0 / (1.0 + 2.0 * ratio / 3.0)
tail = green * 25.0 / 36.0
centre = green * (7.0 / 9.0 + ratio / 18.0)
MESH = pl.DeviceIdType.MESH
f32 = jnp.float32
bf16 = jnp.bfloat16
PAD = 8
LOAD_PARTS = 2
BATCH = 8
EDGE_ROWS = 64
BLOCK = 16
PER_TILE = 6
STRETCH = 1.8203296661376953


def powers_of_ratio(exponent, bits):
    value = jnp.ones(exponent.shape, f32)
    for bit in range(bits):
        factor = float(ratio ** (2**bit))
        factor = factor if abs(factor) > 1e-37 else 0.0
        value = value * jnp.where((exponent >> bit) & 1 == 1, factor, 1.0)
    return value


def halves(values):
    high = values.astype(bf16)
    return high, (values - high.astype(f32)).astype(bf16)


def band_matrix(points):
    source = lax.broadcasted_iota(jnp.int32, (points, points), 0)
    target = lax.broadcasted_iota(jnp.int32, (points, points), 1)
    distance = jnp.abs(target - source - 1)
    values = jnp.where(distance == 0, centre, tail * powers_of_ratio(distance, 7))
    return jnp.where((source < points - 2) & (distance < 128), values, 0.0)


def correction_matrix(points):
    half = points // 2
    source = lax.broadcasted_iota(jnp.int32, (points, points), 0)
    target = lax.broadcasted_iota(jnp.int32, (points, points), 1)
    distance = jnp.where(source < half, target, points - 1 - target)
    edge = jnp.where(distance == 0, 1.0, 0.0)
    decay = jnp.where(distance < 128, STRETCH * powers_of_ratio(distance, 7), 0.0)
    return jnp.where(source % 2 == 1, edge, decay), source


def ring(axis):
    count = lax.axis_size(axis)
    me = lax.axis_index(axis)
    return lax.rem(me + 1, count), lax.rem(me + count - 1, count)


def local_kernel(
    velocity, metric_y, local, sheared, strips, spreads,
    my_line, band, held, sent, own, arrived,
    my_sem, in_sem, y_send, y_recv, x_send, x_recv,
):
    fields, depth, rows, points = velocity.shape
    half = points // 2
    right, left = ring("gx")
    above, below = ring("gy")
    planes = depth // LOAD_PARTS

    barrier = pltpu.get_barrier_semaphore()
    for axis, place in (("gx", right), ("gx", left), ("gy", above), ("gy", below)):
        pl.semaphore_signal(barrier, inc=1, device_id={axis: place}, device_id_type=MESH)

    def load(part):
        field = part // LOAD_PARTS
        span = pl.ds((part % LOAD_PARTS) * planes, planes)
        return [
            pltpu.make_async_copy(
                velocity.at[field, span, :, side * half : (side + 1) * half],
                held.at[field, side, span, PAD : PAD + rows],
                in_sem.at[part, side],
            )
            for side in range(2)
        ]

    for part in range(fields * LOAD_PARTS):
        for copy in load(part):
            copy.start()
    my_load = pltpu.make_async_copy(metric_y, my_line, my_sem)
    my_load.start()

    high, low = halves(band_matrix(points))
    band[0:points] = high
    band[points : 2 * points] = high
    band[2 * points :] = low
    decay, source = correction_matrix(points)
    for z in range(depth):
        spreads[z] = jnp.where(source // 2 % depth == z, decay, 0.0).astype(bf16)

    lane = lax.broadcasted_iota(jnp.int32, (8, half), 1)
    odd = lane % 2 == 1
    scale = tail * (1.0 + ratio)
    spread = scale * (1.0 - ratio)
    left_weight = jnp.where(lane == 0, -scale * ratio, spread * powers_of_ratio(lane, 7))
    right_weight = jnp.where(
        lane == half - 1, scale * ratio, -spread * powers_of_ratio(half - 1 - lane, 7)
    )

    wide_odd = lax.broadcasted_iota(jnp.int32, (EDGE_ROWS // 8, 8, half), 2) % 2
    edge_lanes = (1 - wide_odd, half - 2 + wide_odd)

    def edges(part, carry):
        for copy in load(part):
            copy.wait()
        field = part // LOAD_PARTS

        def plane(step, carry):
            z = (part % LOAD_PARTS) * planes + step
            masks = [lane // 2 == within * 8 + z for within in range(PER_TILE)]
            for start in range(0, rows, EDGE_ROWS):
                for side, weight in ((0, left_weight), (1, right_weight)):
                    block = held[field, side, z, PAD + start : PAD + start + EDGE_ROWS, :]
                    block = block.reshape(EDGE_ROWS // 8, 8, half)
                    edge = jnp.take_along_axis(block, edge_lanes[side], axis=2)
                    total = jnp.sum(block * weight, axis=2, keepdims=True)
                    value = jnp.where(odd, edge, total)
                    for index in range(EDGE_ROWS // 8):
                        group = start // 8 + index
                        tile, within = divmod(group // 2, PER_TILE)
                        place = (side, field, tile, pl.ds((group % 2) * 8, 8))
                        pltpu.store(sent.at[place], value[index], mask=masks[within])
                        pltpu.store(own.at[place], edge[index], mask=masks[within])
            return carry

        return lax.fori_loop(0, planes, plane, carry)

    lax.fori_loop(0, fields * LOAD_PARTS, edges, 0)

    pl.semaphore_wait(barrier, 4)
    x_copies = [
        pltpu.make_async_remote_copy(
            sent.at[side], arrived.at[1 - side], x_send.at[side], x_recv.at[1 - side],
            device_id={"gx": place}, device_id_type=MESH,
        )
        for side, place in ((0, left), (1, right))
    ]
    y_copies = [
        pltpu.make_async_remote_copy(
            velocity.at[0, :, first : first + PAD, side * half : (side + 1) * half],
            held.at[0, side, :, target : target + PAD],
            y_send.at[way, side], y_recv.at[way, side],
            device_id={"gy": place}, device_id_type=MESH,
        )
        for way, (first, target, place) in enumerate(
            ((rows - PAD, 0, above), (0, rows + PAD, below))
        )
        for side in range(2)
    ]
    for copy in x_copies + y_copies:
        copy.start()

    many = BATCH * rows
    def product(index, carry):
        field = index // (depth // BATCH)
        z = (index % (depth // BATCH)) * BATCH
        first = held[field, 0, pl.ds(z, BATCH), PAD : PAD + rows, :].reshape(many, half)
        second = held[field, 1, pl.ds(z, BATCH), PAD : PAD + rows, :].reshape(many, half)
        step = pltpu.roll(jnp.concatenate([first, second], axis=1), points - 2, 1)
        step = step - jnp.concatenate([first, second], axis=1)
        high, low = halves(step)
        result = jnp.dot(
            jnp.concatenate([high, low, high], axis=1), band[...], preferred_element_type=f32
        )
        local[field, pl.ds(z, BATCH)] = result.reshape(BATCH, rows, points)
        return carry

    lax.fori_loop(0, fields * depth // BATCH, product, 0)

    my_load.wait()
    square = (
        lax.broadcasted_iota(jnp.int32, (rows, rows), 0)
        == lax.broadcasted_iota(jnp.int32, (rows, rows), 1)
    )
    my_row = my_line[...].reshape(1, rows)
    my_column = jnp.sum(jnp.where(square, my_row, 0.0), axis=1, keepdims=True) / 60.0

    for copy in y_copies:
        copy.wait()

    def shear_plane(z, carry):
        for side in range(2):

            def shifted(k):
                return held[0, side, z, PAD + k : rows + PAD + k, :]

            sheared[z, :, side * half : (side + 1) * half] = my_column * (
                45.0 * (shifted(1) - shifted(-1))
                - 9.0 * (shifted(2) - shifted(-2))
                + (shifted(3) - shifted(-3))
            )
        return carry

    lax.fori_loop(0, depth, shear_plane, 0)

    for copy in x_copies:
        copy.wait()
    shape = arrived.shape[1:]
    small_odd = small_lanes(shape) % 2 == 1
    strip_lanes = small_lanes((BLOCK, half)) // BLOCK
    for side in range(2):
        sign = 1.0 if side == 0 else -1.0
        far, near = arrived[side], own[side]
        far_edge = pltpu.roll(far, half - 1, 3)
        straddle = sign * (near - far_edge)
        jump = sign * (pltpu.roll(near, half - 1, 3) - far_edge)
        value = jnp.where(
            small_odd,
            pltpu.roll((centre - tail) * straddle, 1, 3),
            (far + tail * straddle + (tail * ratio) * jump) * (1.0 / STRETCH),
        )
        for field in range(fields):
            for block in range(rows // BLOCK):
                tile, within = divmod(block, PER_TILE)
                start = field * rows + block * BLOCK
                piece = jnp.where(strip_lanes == within, value[field, tile], 0.0)
                high, low = halves(piece)
                strips[start : start + BLOCK, side * half : (side + 1) * half] = high
                strips[start : start + BLOCK, points + side * half : points + (side + 1) * half] = low


def small_lanes(shape):
    return lax.broadcasted_iota(jnp.int32, shape, len(shape) - 1)


def finish_kernel(
    local, sheared, strips, spreads, metric_x, derivs, vorticity, staged, out_sem
):
    fields, depth, rows, points = derivs.shape
    mx = metric_x[...].reshape(1, points)

    def copies(z):
        out = [
            pltpu.make_async_copy(staged.at[field, z], derivs.at[field, z], out_sem.at[field, z])
            for field in range(fields)
        ]
        out.append(pltpu.make_async_copy(staged.at[fields, z], vorticity.at[z], out_sem.at[fields, z]))
        return out

    def plane(z, carry):
        sends = copies(z)
        change = jnp.dot(
            strips[:, :points], spreads[z], preferred_element_type=f32
        ) + jnp.dot(strips[:, points:], spreads[z], preferred_element_type=f32)
        for field in range(fields):
            value = (local[field, z] + change[field * rows : (field + 1) * rows]) * mx
            staged[field, z] = value
            if field == 1:
                staged[fields, z] = value - sheared[z]
        for copy in sends:
            copy.start()
        return carry

    lax.fori_loop(0, depth, plane, 0)

    def drain(z, carry):
        for copy in copies(z):
            copy.wait()
        return carry

    lax.fori_loop(0, depth, drain, 0)


def per_device(velocity, metric_x, metric_y):
    fields, depth, rows, points = velocity.shape
    half = points // 2
    packs = (fields, 2, BLOCK, half)
    parts = fields * LOAD_PARTS
    anywhere = pl.BlockSpec(memory_space=pl.ANY)
    hbm = pl.BlockSpec(memory_space=pltpu.HBM)
    vmem = pl.BlockSpec(memory_space=pltpu.VMEM)
    local, sheared, strips, spreads = pl.pallas_call(
        local_kernel,
        out_shape=(
            pltpu.VMEM((fields, depth, rows, points), f32),
            pltpu.VMEM((depth, rows, points), f32),
            pltpu.VMEM((fields * rows, 2 * points), bf16),
            pltpu.VMEM((depth, points, points), bf16),
        ),
        in_specs=[hbm, hbm],
        out_specs=(vmem,) * 4,
        scratch_shapes=[
            pltpu.VMEM((rows,), f32),
            pltpu.VMEM((3 * points, points), bf16),
            pltpu.VMEM((fields, 2, depth, rows + 2 * PAD, half), f32),
            pltpu.VMEM((2,) + packs, f32),
            pltpu.VMEM((2,) + packs, f32),
            pltpu.VMEM((2,) + packs, f32),
            pltpu.SemaphoreType.DMA(()),
            pltpu.SemaphoreType.DMA((parts, 2)),
            pltpu.SemaphoreType.DMA((2, 2)),
            pltpu.SemaphoreType.DMA((2, 2)),
            pltpu.SemaphoreType.DMA((2,)),
            pltpu.SemaphoreType.DMA((2,)),
        ],
        compiler_params=pltpu.CompilerParams(
            collective_id=0, has_side_effects=True, vmem_limit_bytes=24 * 1024 * 1024
        ),
        name="local",
    )(
        pltpu.with_memory_space_constraint(velocity, pltpu.HBM),
        pltpu.with_memory_space_constraint(metric_y, pltpu.HBM),
    )
    return pl.pallas_call(
        finish_kernel,
        out_shape=(
            jax.ShapeDtypeStruct((fields, depth, rows, points), f32),
            jax.ShapeDtypeStruct((depth, rows, points), f32),
        ),
        in_specs=[vmem] * 5,
        out_specs=(anywhere, anywhere),
        scratch_shapes=[
            pltpu.VMEM((fields + 1, depth, rows, points), f32),
            pltpu.SemaphoreType.DMA((fields + 1, depth)),
        ],
        compiler_params=pltpu.CompilerParams(vmem_limit_bytes=24 * 1024 * 1024),
        name="finish",
    )(local, sheared, strips, spreads, metric_x)


def solution(mesh):
    in_specs = (P(None, None, "gy", "gx"), P("gx"), P("gy"))
    out_specs = (P(None, None, "gy", "gx"), P(None, "gy", "gx"))
    return jax.shard_map(
        per_device, mesh=mesh, in_specs=in_specs, out_specs=out_specs, check_vma=False
    )
```

time: 27.5 us -> 22.2 us (0.81)
  Pallas kernels: 26.8 us -> 21.3 us
    pallas_call x1, Pallas kernels: 21.9 us -> 17.7 us  [per_device(): pl.pallas_call(local_kernel, out_shape=(pltpu.VMEM((fields, depth, rows,...]
    pallas_call x1, Pallas kernels: 4.92 us -> 3.67 us  [per_device(): pl.pallas_call(finish_kernel, out_shape=(jax.ShapeDtypeStruct((fields, de...]
where the time goes in v2:
time: 22.2 us; the launch traced here: 22 us
  Pallas kernels  21.3 us (96%)
  between operations  0.65 us (3%)
    pallas_call x1, Pallas kernels, per_device(): pl.pallas_call(local_kernel, out_shape=(pltpu.VMEM((fields, depth, rows,...  17.7 us
    pallas_call x1, Pallas kernels, per_device(): pl.pallas_call(finish_kernel, out_shape=(jax.ShapeDtypeStruct((fields, de...  3.67 us

profile of v2, /device:TPU:1, one launch (start us, length us, event | category | flops | bytes accessed | tf_op | source)
XLA Modules:
  0.0 22.0 jit_solution(10542146955535937839)
XLA Ops:
  0.6 0.0 copy-start
  0.6 17.7 %local.1 = (f32[3,8,192,256]{3,2,1,0:T(8,128)S(1)}, f32[8,192,256]{2,1,0:T(8,128)S(1)}, bf16[576,512]{1,0:T(8,128)(2,1)S(1)}, bf16[8,256,256]{2,1,0:T(8,128)(2,1)S(1)}) custom-call(f32[3,8,192,256]{3,2,1,0:T(8,128)} %velocity.1, f32[192]{0:T(256)} %metric_y.1), custom_call_target="tpu_custom_call" | custom-call | tf_op jit(solution)/shard_map/local/pallas_call | solution.py:285
  18.3 0.0 copy-done
  18.3 3.7 %finish.1 = (f32[3,8,192,256]{3,2,1,0:T(8,128)}, f32[8,192,256]{2,1,0:T(8,128)}) custom-call(f32[3,8,192,256]{3,2,1,0:T(8,128)S(1)} %get-tuple-element.6.local, f32[8,192,256]{2,1,0:T(8,128)S(1)} %get-tuple-element.7.sheared, bf16[576,512]{1,0:T(8,128)(2,1)S(1)} %get-tuple-element.8.strips, bf16[8,256,256]{2,1,0:T(8,128)(2,1)S(1)} %get-tuple-element.9.spreads, ...), custom_call_target="tpu_custom_call" | custom-call | tf_op jit(solution)/shard_map/finish/pallas_call | solution.py:317
Async XLA Ops:
  0.6 17.7 %copy-start = (f32[256]{0:T(256)S(1)}, f32[256]{0:T(256)}, u32[]{:S(2)}) copy-start(f32[256]{0:T(256)} %metric_x.1) | copy-start | bytes 3076

commit v3 on v2

v3 whole, which is shorter than its diff:
```python
import numpy as np
import jax
import jax.numpy as jnp
from jax import lax
from jax.experimental import pallas as pl
from jax.experimental.pallas import tpu as pltpu
from jax.sharding import PartitionSpec as P

ratio = (np.sqrt(5.0) - 3.0) / 2.0
green = 1.0 / (1.0 + 2.0 * ratio / 3.0)
tail = green * 25.0 / 36.0
centre = green * (7.0 / 9.0 + ratio / 18.0)
MESH = pl.DeviceIdType.MESH
f32 = jnp.float32
bf16 = jnp.bfloat16
PAD = 8
LOAD_PARTS = 2
BATCH = 8
EDGE_PLANES = 2
MEET = 1
FINISH_PLANES = 2
BLOCK = 16
PER_TILE = 6
STRETCH = 1.8203296661376953


def powers_of_ratio(exponent, bits):
    value = jnp.ones(exponent.shape, f32)
    for bit in range(bits):
        factor = float(ratio ** (2**bit))
        factor = factor if abs(factor) > 1e-37 else 0.0
        value = value * jnp.where((exponent >> bit) & 1 == 1, factor, 1.0)
    return value


def halves(values):
    high = values.astype(bf16)
    return high, (values - high.astype(f32)).astype(bf16)


def band_matrix(points):
    source = lax.broadcasted_iota(jnp.int32, (points, points), 0)
    target = lax.broadcasted_iota(jnp.int32, (points, points), 1)
    distance = jnp.abs(target - source - 1)
    values = jnp.where(distance == 0, centre, tail * powers_of_ratio(distance, 7))
    return jnp.where((source < points - 2) & (distance < 128), values, 0.0)


def correction_matrix(points):
    half = points // 2
    source = lax.broadcasted_iota(jnp.int32, (points, points), 0)
    target = lax.broadcasted_iota(jnp.int32, (points, points), 1)
    distance = jnp.where(source < half, target, points - 1 - target)
    edge = jnp.where(distance == 0, 1.0, 0.0)
    decay = jnp.where(distance < 128, STRETCH * powers_of_ratio(distance, 7), 0.0)
    second = source % 2 == jnp.where(source < half, 1, 0)
    return jnp.where(second, edge, decay), source


def ring(axis):
    count = lax.axis_size(axis)
    me = lax.axis_index(axis)
    return lax.rem(me + 1, count), lax.rem(me + count - 1, count)


def local_kernel(
    velocity, metric_y, local, sheared, strips, spreads,
    my_line, band, held, sent, own, arrived,
    ready, my_sem, in_sem, y_send, y_recv, x_send, x_recv,
):
    fields, depth, rows, points = velocity.shape
    half = points // 2
    right, left = ring("gx")
    above, below = ring("gy")
    seam = lax.axis_index("gx") == 0
    last = lax.axis_index("gx") == lax.axis_size("gx") - 1
    barrier = pltpu.get_barrier_semaphore()
    for axis, place in (("gy", above), ("gy", below), ("gx", left)):
        pl.semaphore_signal(barrier, inc=1, device_id={axis: place}, device_id_type=MESH)

    @pl.when(jnp.logical_not(last))
    def greet_right():
        pl.semaphore_signal(barrier, inc=1, device_id={"gx": right}, device_id_type=MESH)

    planes = depth // LOAD_PARTS

    def load(side, part):
        field = part // LOAD_PARTS
        span = pl.ds((part % LOAD_PARTS) * planes, planes)
        return pltpu.make_async_copy(
            velocity.at[field, span, :, side * half : (side + 1) * half],
            held.at[field, side, span, PAD : PAD + rows],
            in_sem.at[side, part],
        )

    parts = fields * LOAD_PARTS
    for part in range(parts):
        load(1, part).start()
    my_load = pltpu.make_async_copy(metric_y, my_line, my_sem)

    high, low = halves(band_matrix(points))
    band[0:points] = high
    band[points : 2 * points] = high
    band[2 * points :] = low

    lane = lax.broadcasted_iota(jnp.int32, (8, half), 1)
    odd = lane % 2 == 1
    scale = tail * (1.0 + ratio)
    spread = scale * (1.0 - ratio)
    left_weight = jnp.where(lane == 0, -scale * ratio, spread * powers_of_ratio(lane, 7))
    right_weight = jnp.where(
        lane == half - 1, scale * ratio, -spread * powers_of_ratio(half - 1 - lane, 7)
    )

    def edges(side, after):
        weight = right_weight if side else left_weight

        def piece(part, carry):
            load(side, part).wait()
            if side:

                @pl.when(part == parts - 2)
                def start_others():
                    for other in range(parts):
                        load(0, other).start()
                    my_load.start()

            field = part // LOAD_PARTS

            def pair(step, carry):
                first = (part % LOAD_PARTS) * planes + step * EDGE_PLANES
                for z in [first + k for k in range(EDGE_PLANES)]:
                    groups = range(rows // 8)
                    blocks = [held[field, side, z, PAD + g * 8 : PAD + g * 8 + 8, :] for g in groups]
                    totals = [jnp.sum(block * weight, axis=1, keepdims=True) for block in blocks]
                    masks = [lane // 2 == within * 8 + z for within in range(PER_TILE)]
                    for group, block, total in zip(groups, blocks, totals):
                        tile, within = divmod(group // 2, PER_TILE)
                        edge = pltpu.roll(block, within * BLOCK + 2 * z + 2 * side, 1)
                        value = jnp.where(odd, edge, total) if side else jnp.where(odd, total, edge)
                        place = (side, field, tile, pl.ds((group % 2) * 8, 8))
                        pltpu.store(sent.at[place], value, mask=masks[within])
                        pltpu.store(own.at[place], edge, mask=masks[within])
                return carry

            return lax.fori_loop(0, planes // EDGE_PLANES, pair, carry)

        def whole(field, carry):
            lax.fori_loop(field * LOAD_PARTS, (field + 1) * LOAD_PARTS, piece, 0)
            after(field)
            return carry

        lax.fori_loop(0, fields, whole, 0)

    def x_copy(side, field):
        return pltpu.make_async_remote_copy(
            sent.at[side, field], arrived.at[1 - side, field],
            x_send.at[side, field], x_recv.at[1 - side, field],
            device_id={"gx": right if side else left}, device_id_type=MESH,
        )

    y_copies = [
        pltpu.make_async_remote_copy(
            velocity.at[0, :, first : first + PAD, side * half : (side + 1) * half],
            held.at[0, side, :, target : target + PAD],
            y_send.at[way, side], y_recv.at[way, side],
            device_id={"gy": place}, device_id_type=MESH,
        )
        for way, (first, target, place) in enumerate(
            ((rows - PAD, 0, above), (0, rows + PAD, below))
        )
        for side in range(2)
    ]

    def send_right(field):
        @pl.when(field == MEET)
        def meet():
            @pl.when(seam)
            def meet_three():
                pl.semaphore_wait(barrier, 3)

            @pl.when(jnp.logical_not(seam))
            def meet_four():
                pl.semaphore_wait(barrier, 4)

            @pl.when(last)
            def invite():
                pl.semaphore_signal(ready, inc=1, device_id={"gx": right}, device_id_type=MESH)

            for earlier in range(MEET):
                x_copy(1, earlier).start()

        @pl.when(field >= MEET)
        def send():
            x_copy(1, field).start()

    def send_left(field):
        @pl.when(field == 0)
        def first():
            for copy in y_copies:
                copy.start()

        @pl.when(jnp.logical_not(seam))
        def send():
            x_copy(0, field).start()

    edges(1, send_right)
    edges(0, send_left)

    decay, source = correction_matrix(points)
    for z in range(depth):
        spreads[z] = jnp.where(source // 2 % depth == z, decay, 0.0).astype(bf16)

    many = BATCH * rows
    def product(index, carry):
        field = index // (depth // BATCH)
        z = (index % (depth // BATCH)) * BATCH
        first = held[field, 0, pl.ds(z, BATCH), PAD : PAD + rows, :].reshape(many, half)
        second = held[field, 1, pl.ds(z, BATCH), PAD : PAD + rows, :].reshape(many, half)
        step = pltpu.roll(jnp.concatenate([first, second], axis=1), points - 2, 1)
        step = step - jnp.concatenate([first, second], axis=1)
        high, low = halves(step)
        result = jnp.dot(
            jnp.concatenate([high, low, high], axis=1), band[...], preferred_element_type=f32
        )
        local[field, pl.ds(z, BATCH)] = result.reshape(BATCH, rows, points)
        return carry

    my_load.wait()
    square = (
        lax.broadcasted_iota(jnp.int32, (rows, rows), 0)
        == lax.broadcasted_iota(jnp.int32, (rows, rows), 1)
    )
    my_row = my_line[...].reshape(1, rows)
    my_column = jnp.sum(jnp.where(square, my_row, 0.0), axis=1, keepdims=True) / 60.0

    def shear_rows(z, start, stop):
        for side in range(2):

            def shifted(k):
                return held[0, side, z, PAD + start + k : PAD + stop + k, :]

            sheared[z, start:stop, side * half : (side + 1) * half] = my_column[start:stop] * (
                45.0 * (shifted(1) - shifted(-1))
                - 9.0 * (shifted(2) - shifted(-2))
                + (shifted(3) - shifted(-3))
            )

    def shear_inner(z, carry):
        shear_rows(z, PAD, rows - PAD)
        return carry

    lax.fori_loop(0, depth, shear_inner, 0)

    lax.fori_loop(0, fields * depth // BATCH, product, 0)

    @pl.when(seam)
    def send_late():
        pl.semaphore_wait(ready, 1)
        for field in range(fields):
            x_copy(0, field).start()

    for copy in y_copies:
        copy.wait()

    for z in range(depth):
        shear_rows(z, 0, PAD)
        shear_rows(z, rows - PAD, rows)

    shape = arrived.shape[1:]
    small_odd = small_lanes(shape) % 2 == 1
    strip_lanes = small_lanes((BLOCK, half)) // BLOCK
    for side in (1, 0):
        for field in range(fields):
            x_copy(1 - side, field).wait_recv()
        far, near = arrived[side], own[side]
        turn, sign = (half - 1, 1.0) if side == 0 else (1, -1.0)
        straddle = sign * (near - far)
        jump = sign * (near - pltpu.roll(far, turn, 3))
        value = jnp.where(
            small_odd == (side == 0),
            (centre - tail) * straddle,
            (far + tail * pltpu.roll(straddle, turn, 3) + (tail * ratio) * jump)
            * (1.0 / STRETCH),
        )
        for field in range(fields):
            for block in range(rows // BLOCK):
                tile, within = divmod(block, PER_TILE)
                start = field * rows + block * BLOCK
                piece = jnp.where(strip_lanes == within, value[field, tile], 0.0)
                high, low = halves(piece)
                strips[start : start + BLOCK, side * half : (side + 1) * half] = high
                strips[start : start + BLOCK, points + side * half : points + (side + 1) * half] = low
    for side in range(2):
        for field in range(fields):
            x_copy(side, field).wait_send()


def small_lanes(shape):
    return lax.broadcasted_iota(jnp.int32, shape, len(shape) - 1)


def finish_kernel(
    local, sheared, strips, spreads, metric_x, derivs, vorticity, staged, out_sem
):
    fields, depth, rows, points = derivs.shape
    mx = metric_x[...].reshape(1, points)

    def copies(z):
        out = [
            pltpu.make_async_copy(staged.at[field, z], derivs.at[field, z], out_sem.at[0])
            for field in range(fields)
        ]
        out.append(pltpu.make_async_copy(staged.at[fields, z], vorticity.at[z], out_sem.at[1]))
        return out

    def planes(step, carry):
        for z in [step * FINISH_PLANES + k for k in range(FINISH_PLANES)]:
            change = jnp.dot(
                strips[:, :points], spreads[z], preferred_element_type=f32
            ) + jnp.dot(strips[:, points:], spreads[z], preferred_element_type=f32)
            for field in range(fields):
                value = (local[field, z] + change[field * rows : (field + 1) * rows]) * mx
                staged[field, z] = value
                if field == 1:
                    staged[fields, z] = value - sheared[z]
            for copy in copies(z):
                copy.start()
        return carry

    lax.fori_loop(0, depth // FINISH_PLANES, planes, 0)

    pltpu.make_async_copy(staged.at[0:fields], derivs, out_sem.at[0]).wait()
    pltpu.make_async_copy(staged.at[fields], vorticity, out_sem.at[1]).wait()


def per_device(velocity, metric_x, metric_y):
    fields, depth, rows, points = velocity.shape
    half = points // 2
    packs = (fields, 2, BLOCK, half)
    parts = fields * LOAD_PARTS
    anywhere = pl.BlockSpec(memory_space=pl.ANY)
    hbm = pl.BlockSpec(memory_space=pltpu.HBM)
    vmem = pl.BlockSpec(memory_space=pltpu.VMEM)
    local, sheared, strips, spreads = pl.pallas_call(
        local_kernel,
        out_shape=(
            pltpu.VMEM((fields, depth, rows, points), f32),
            pltpu.VMEM((depth, rows, points), f32),
            pltpu.VMEM((fields * rows, 2 * points), bf16),
            pltpu.VMEM((depth, points, points), bf16),
        ),
        in_specs=[hbm, hbm],
        out_specs=(vmem,) * 4,
        scratch_shapes=[
            pltpu.VMEM((rows,), f32),
            pltpu.VMEM((3 * points, points), bf16),
            pltpu.VMEM((fields, 2, depth, rows + 2 * PAD, half), f32),
            pltpu.VMEM((2,) + packs, f32),
            pltpu.VMEM((2,) + packs, f32),
            pltpu.VMEM((2,) + packs, f32),
            pltpu.SemaphoreType.REGULAR,
            pltpu.SemaphoreType.DMA(()),
            pltpu.SemaphoreType.DMA((2, parts)),
            pltpu.SemaphoreType.DMA((2, 2)),
            pltpu.SemaphoreType.DMA((2, 2)),
            pltpu.SemaphoreType.DMA((2, fields)),
            pltpu.SemaphoreType.DMA((2, fields)),
        ],
        compiler_params=pltpu.CompilerParams(
            collective_id=0, has_side_effects=True, vmem_limit_bytes=24 * 1024 * 1024
        ),
        name="local",
    )(
        pltpu.with_memory_space_constraint(velocity, pltpu.HBM),
        pltpu.with_memory_space_constraint(metric_y, pltpu.HBM),
    )
    return pl.pallas_call(
        finish_kernel,
        out_shape=(
            jax.ShapeDtypeStruct((fields, depth, rows, points), f32),
            jax.ShapeDtypeStruct((depth, rows, points), f32),
        ),
        in_specs=[vmem] * 5,
        out_specs=(anywhere, anywhere),
        scratch_shapes=[
            pltpu.VMEM((fields + 1, depth, rows, points), f32),
            pltpu.SemaphoreType.DMA((2,)),
        ],
        compiler_params=pltpu.CompilerParams(vmem_limit_bytes=24 * 1024 * 1024),
        name="finish",
    )(local, sheared, strips, spreads, metric_x)


def solution(mesh):
    in_specs = (P(None, None, "gy", "gx"), P("gx"), P("gy"))
    out_specs = (P(None, None, "gy", "gx"), P(None, "gy", "gx"))
    return jax.shard_map(
        per_device, mesh=mesh, in_specs=in_specs, out_specs=out_specs, check_vma=False
    )
```

time: 22.2 us -> 18.5 us (0.83)
  Pallas kernels: 21.3 us -> 17.8 us
    pallas_call x1, Pallas kernels: 17.7 us -> 14.5 us  [per_device(): pl.pallas_call(local_kernel, out_shape=(pltpu.VMEM((fields, depth, rows,...]
    pallas_call x1, Pallas kernels: 3.67 us -> 3.24 us  [per_device(): pl.pallas_call(finish_kernel, out_shape=(jax.ShapeDtypeStruct((fields, de...]
where the time goes in v3:
time: 18.5 us; the launch traced here: 18.4 us
  Pallas kernels  17.8 us (96%)
  between operations  0.65 us (4%)
    pallas_call x1, Pallas kernels, per_device(): pl.pallas_call(local_kernel, out_shape=(pltpu.VMEM((fields, depth, rows,...  14.5 us
    pallas_call x1, Pallas kernels, per_device(): pl.pallas_call(finish_kernel, out_shape=(jax.ShapeDtypeStruct((fields, de...  3.24 us

profile of v3, /device:TPU:1, one launch (start us, length us, event | category | flops | bytes accessed | tf_op | source)
XLA Modules:
  0.0 18.4 jit_solution(7951962704077374582)
XLA Ops:
  0.6 0.0 copy-start
  0.6 14.5 %local.1 = (f32[3,8,192,256]{3,2,1,0:T(8,128)S(1)}, f32[8,192,256]{2,1,0:T(8,128)S(1)}, bf16[576,512]{1,0:T(8,128)(2,1)S(1)}, bf16[8,256,256]{2,1,0:T(8,128)(2,1)S(1)}) custom-call(f32[3,8,192,256]{3,2,1,0:T(8,128)} %velocity.1, f32[192]{0:T(256)} %metric_y.1), custom_call_target="tpu_custom_call" | custom-call | tf_op jit(solution)/shard_map/local/pallas_call | solution.py:345
  15.2 0.0 copy-done
  15.2 3.2 %finish.1 = (f32[3,8,192,256]{3,2,1,0:T(8,128)}, f32[8,192,256]{2,1,0:T(8,128)}) custom-call(f32[3,8,192,256]{3,2,1,0:T(8,128)S(1)} %get-tuple-element.6.local, f32[8,192,256]{2,1,0:T(8,128)S(1)} %get-tuple-element.7.sheared, bf16[576,512]{1,0:T(8,128)(2,1)S(1)} %get-tuple-element.8.strips, bf16[8,256,256]{2,1,0:T(8,128)(2,1)S(1)} %get-tuple-element.9.spreads, ...), custom_call_target="tpu_custom_call" | custom-call | tf_op jit(solution)/shard_map/finish/pallas_call | solution.py:378
Async XLA Ops:
  0.6 14.5 %copy-start = (f32[256]{0:T(256)S(1)}, f32[256]{0:T(256)}, u32[]{:S(2)}) copy-start(f32[256]{0:T(256)} %metric_x.1) | copy-start | bytes 3076

commit v4 on v3

--- a/solution.py
+++ b/solution.py
@@ -16,9 +16,9 @@
 PAD = 8
 LOAD_PARTS = 2
 BATCH = 8
-EDGE_PLANES = 2
+EDGE_PLANES = 4
 MEET = 1
-FINISH_PLANES = 2
+FINISH_PLANES = 4
 BLOCK = 16
 PER_TILE = 6
 STRETCH = 1.8203296661376953
@@ -74,14 +74,6 @@
     above, below = ring("gy")
     seam = lax.axis_index("gx") == 0
     last = lax.axis_index("gx") == lax.axis_size("gx") - 1
-    barrier = pltpu.get_barrier_semaphore()
-    for axis, place in (("gy", above), ("gy", below), ("gx", left)):
-        pl.semaphore_signal(barrier, inc=1, device_id={axis: place}, device_id_type=MESH)
-
-    @pl.when(jnp.logical_not(last))
-    def greet_right():
-        pl.semaphore_signal(barrier, inc=1, device_id={"gx": right}, device_id_type=MESH)
-
     planes = depth // LOAD_PARTS
 
     def load(side, part):
@@ -96,6 +88,14 @@
     parts = fields * LOAD_PARTS
     for part in range(parts):
         load(1, part).start()
+    barrier = pltpu.get_barrier_semaphore()
+    for axis, place in (("gy", above), ("gy", below), ("gx", left)):
+        pl.semaphore_signal(barrier, inc=1, device_id={axis: place}, device_id_type=MESH)
+
+    @pl.when(jnp.logical_not(last))
+    def greet_right():
+        pl.semaphore_signal(barrier, inc=1, device_id={"gx": right}, device_id_type=MESH)
+
     my_load = pltpu.make_async_copy(metric_y, my_line, my_sem)
 
     high, low = halves(band_matrix(points))
@@ -267,27 +267,26 @@
         shear_rows(z, 0, PAD)
         shear_rows(z, rows - PAD, rows)
 
-    shape = arrived.shape[1:]
+    shape = arrived.shape[2:]
     small_odd = small_lanes(shape) % 2 == 1
     strip_lanes = small_lanes((BLOCK, half)) // BLOCK
     for side in (1, 0):
+        turn, sign = (half - 1, 1.0) if side == 0 else (1, -1.0)
         for field in range(fields):
             x_copy(1 - side, field).wait_recv()
-        far, near = arrived[side], own[side]
-        turn, sign = (half - 1, 1.0) if side == 0 else (1, -1.0)
-        straddle = sign * (near - far)
-        jump = sign * (near - pltpu.roll(far, turn, 3))
-        value = jnp.where(
-            small_odd == (side == 0),
-            (centre - tail) * straddle,
-            (far + tail * pltpu.roll(straddle, turn, 3) + (tail * ratio) * jump)
-            * (1.0 / STRETCH),
-        )
-        for field in range(fields):
+            far, near = arrived[side, field], own[side, field]
+            straddle = sign * (near - far)
+            jump = sign * (near - pltpu.roll(far, turn, 2))
+            value = jnp.where(
+                small_odd == (side == 0),
+                (centre - tail) * straddle,
+                (far + tail * pltpu.roll(straddle, turn, 2) + (tail * ratio) * jump)
+                * (1.0 / STRETCH),
+            )
             for block in range(rows // BLOCK):
                 tile, within = divmod(block, PER_TILE)
                 start = field * rows + block * BLOCK
-                piece = jnp.where(strip_lanes == within, value[field, tile], 0.0)
+                piece = jnp.where(strip_lanes == within, value[tile], 0.0)
                 high, low = halves(piece)
                 strips[start : start + BLOCK, side * half : (side + 1) * half] = high
                 strips[start : start + BLOCK, points + side * half : points + (side + 1) * half] = low
@@ -316,15 +315,17 @@
 
     def planes(step, carry):
         for z in [step * FINISH_PLANES + k for k in range(FINISH_PLANES)]:
-            change = jnp.dot(
-                strips[:, :points], spreads[z], preferred_element_type=f32
-            ) + jnp.dot(strips[:, points:], spreads[z], preferred_element_type=f32)
+            sends = copies(z)
             for field in range(fields):
-                value = (local[field, z] + change[field * rows : (field + 1) * rows]) * mx
+                span = slice(field * rows, (field + 1) * rows)
+                change = jnp.dot(
+                    strips[span, :points], spreads[z], preferred_element_type=f32
+                ) + jnp.dot(strips[span, points:], spreads[z], preferred_element_type=f32)
+                value = (local[field, z] + change) * mx
                 staged[field, z] = value
                 if field == 1:
                     staged[fields, z] = value - sheared[z]
-            for copy in copies(z):
+            for copy in sends:
                 copy.start()
         return carry
 

time: 18.5 us -> 17.8 us (0.962)
  Pallas kernels: 17.8 us -> 17 us
    pallas_call x1, Pallas kernels: 14.5 us -> 14 us  [per_device(): pl.pallas_call(local_kernel, out_shape=(pltpu.VMEM((fields, depth, rows,...]
    pallas_call x1, Pallas kernels: 3.24 us -> 3.02 us  [per_device(): pl.pallas_call(finish_kernel, out_shape=(jax.ShapeDtypeStruct((fields, de...]
where the time goes in v4:
time: 17.8 us; the launch traced here: 17.7 us
  Pallas kernels  17 us (96%)
  between operations  0.65 us (4%)
    pallas_call x1, Pallas kernels, per_device(): pl.pallas_call(local_kernel, out_shape=(pltpu.VMEM((fields, depth, rows,...  14 us
    pallas_call x1, Pallas kernels, per_device(): pl.pallas_call(finish_kernel, out_shape=(jax.ShapeDtypeStruct((fields, de...  3.02 us

profile of v4, /device:TPU:1, one launch (start us, length us, event | category | flops | bytes accessed | tf_op | source)
XLA Modules:
  0.0 17.7 jit_solution(11350312185681531326)
XLA Ops:
  0.6 0.0 copy-start
  0.6 14.0 %local.1 = (f32[3,8,192,256]{3,2,1,0:T(8,128)S(1)}, f32[8,192,256]{2,1,0:T(8,128)S(1)}, bf16[576,512]{1,0:T(8,128)(2,1)S(1)}, bf16[8,256,256]{2,1,0:T(8,128)(2,1)S(1)}) custom-call(f32[3,8,192,256]{3,2,1,0:T(8,128)} %velocity.1, f32[192]{0:T(256)} %metric_y.1), custom_call_target="tpu_custom_call" | custom-call | tf_op jit(solution)/shard_map/local/pallas_call | solution.py:346
  14.7 0.0 copy-done
  14.7 3.0 %finish.1 = (f32[3,8,192,256]{3,2,1,0:T(8,128)}, f32[8,192,256]{2,1,0:T(8,128)}) custom-call(f32[3,8,192,256]{3,2,1,0:T(8,128)S(1)} %get-tuple-element.6.local, f32[8,192,256]{2,1,0:T(8,128)S(1)} %get-tuple-element.7.sheared, bf16[576,512]{1,0:T(8,128)(2,1)S(1)} %get-tuple-element.8.strips, bf16[8,256,256]{2,1,0:T(8,128)(2,1)S(1)} %get-tuple-element.9.spreads, ...), custom_call_target="tpu_custom_call" | custom-call | tf_op jit(solution)/shard_map/finish/pallas_call | solution.py:379
Async XLA Ops:
  0.6 14.0 %copy-start = (f32[256]{0:T(256)S(1)}, f32[256]{0:T(256)}, u32[]{:S(2)}) copy-start(f32[256]{0:T(256)} %metric_x.1) | copy-start | bytes 3076

commit v5 on v4

--- a/solution.py
+++ b/solution.py
@@ -117,14 +117,6 @@
 
         def piece(part, carry):
             load(side, part).wait()
-            if side:
-
-                @pl.when(part == parts - 2)
-                def start_others():
-                    for other in range(parts):
-                        load(0, other).start()
-                    my_load.start()
-
             field = part // LOAD_PARTS
 
             def pair(step, carry):
@@ -204,6 +196,9 @@
         def send():
             x_copy(0, field).start()
 
+    for part in range(parts):
+        load(0, part).start()
+    my_load.start()
     edges(1, send_right)
     edges(0, send_left)
 

time: 17.8 us -> 17.6 us (0.989)
  Pallas kernels: 17 us -> 16.8 us
    pallas_call x1, Pallas kernels: 14 us -> 13.8 us  [per_device(): pl.pallas_call(local_kernel, out_shape=(pltpu.VMEM((fields, depth, rows,...]
where the time goes in v5:
time: 17.6 us; the launch traced here: 17.5 us
  Pallas kernels  16.8 us (95%)
  between operations  0.65 us (4%)
    pallas_call x1, Pallas kernels, per_device(): pl.pallas_call(local_kernel, out_shape=(pltpu.VMEM((fields, depth, rows,...  13.8 us
    pallas_call x1, Pallas kernels, per_device(): pl.pallas_call(finish_kernel, out_shape=(jax.ShapeDtypeStruct((fields, de...  3.02 us

profile of v5, /device:TPU:1, one launch (start us, length us, event | category | flops | bytes accessed | tf_op | source)
XLA Modules:
  0.0 17.5 jit_solution(10099622273322098631)
XLA Ops:
  0.6 0.0 copy-start
  0.6 13.8 %local.1 = (f32[3,8,192,256]{3,2,1,0:T(8,128)S(1)}, f32[8,192,256]{2,1,0:T(8,128)S(1)}, bf16[576,512]{1,0:T(8,128)(2,1)S(1)}, bf16[8,256,256]{2,1,0:T(8,128)(2,1)S(1)}) custom-call(f32[3,8,192,256]{3,2,1,0:T(8,128)} %velocity.1, f32[192]{0:T(256)} %metric_y.1), custom_call_target="tpu_custom_call" | custom-call | tf_op jit(solution)/shard_map/local/pallas_call | solution.py:341
  14.4 0.0 copy-done
  14.5 3.0 %finish.1 = (f32[3,8,192,256]{3,2,1,0:T(8,128)}, f32[8,192,256]{2,1,0:T(8,128)}) custom-call(f32[3,8,192,256]{3,2,1,0:T(8,128)S(1)} %get-tuple-element.6.local, f32[8,192,256]{2,1,0:T(8,128)S(1)} %get-tuple-element.7.sheared, bf16[576,512]{1,0:T(8,128)(2,1)S(1)} %get-tuple-element.8.strips, bf16[8,256,256]{2,1,0:T(8,128)(2,1)S(1)} %get-tuple-element.9.spreads, ...), custom_call_target="tpu_custom_call" | custom-call | tf_op jit(solution)/shard_map/finish/pallas_call | solution.py:374
Async XLA Ops:
  0.6 13.8 %copy-start = (f32[256]{0:T(256)S(1)}, f32[256]{0:T(256)}, u32[]{:S(2)}) copy-start(f32[256]{0:T(256)} %metric_x.1) | copy-start | bytes 3076
